TPU v7x, 32 devices: a whole 2x2x4 slice. The times are simulated.
32 devices in a mesh: dp: 16 (over z, y, core), tensor: 2 (over x).
Axes of the slice: x: 2, y: 2, z: 4, core: 2. Of those that a mesh axis runs over, the one named last changes fastest.
Arguments:
- tokens: bfloat16 [1024, 32, 1024], P('tensor', 'dp'), may hold values from -6 to 6
- d_out: bfloat16 [1024, 32, 1024], P('tensor', 'dp'), may hold values from -6 to 6
- ln1_gain: bfloat16 [1024], P('dp'), may hold values from 0.099609375 to 1.8984375
- ln1_bias: bfloat16 [1024], P('dp'), may hold values from -1.75 to 1.75
- w_qkv: bfloat16 [3, 1024, 1024], P(None, 'dp', 'tensor'), may hold values from -0.1875 to 0.1875
- w_out: bfloat16 [1024, 1024], P('tensor', 'dp'), may hold values from -3 to 3
- ln2_gain: bfloat16 [1024], P('dp'), may hold values from 0.099609375 to 1.8984375
- ln2_bias: bfloat16 [1024], P('dp'), may hold values from -1.75 to 1.75
- w_up: bfloat16 [1024, 4096], P('dp', 'tensor'), may hold values from -0.1875 to 0.1875
- w_down: bfloat16 [4096, 1024], P('tensor', 'dp'), may hold values from -0.09375 to 0.09375
Outputs:
- block_out: bfloat16 [1024, 32, 1024], P('tensor', 'dp')
- input_grad: bfloat16 [1024, 32, 1024], P('tensor', 'dp')
- grad_ln1_gain: float32 [1024], P('dp')
- grad_ln1_bias: float32 [1024], P('dp')
- grad_w_qkv: float32 [3, 1024, 1024], P(None, 'dp', 'tensor')
- grad_w_out: float32 [1024, 1024], P('tensor', 'dp')
- grad_ln2_gain: float32 [1024], P('dp')
- grad_ln2_bias: float32 [1024], P('dp')
- grad_w_up: float32 [1024, 4096], P('dp', 'tensor')
- grad_w_down: float32 [4096, 1024], P('tensor', 'dp')
All inputs are finite; a program needn't handle non-finite values.
Results may differ from a plain program's by a relative error of at most 0.023.
Values may be sent and summed in bfloat16 or wider, within the bound.
No kernel may reach another device: no remote copies, remote signals or barrier semaphores. Data moves between devices by JAX's collectives and lax.ppermute only.
A program may use at most 256 MiB of HBM per device.

v0:
```python
import jax
import jax.numpy as jnp
from jax import lax
from jax.sharding import PartitionSpec as P

HEAD_DIM = 64
EPSILON = 1e-05


def norm_rows(values, norm_gain, norm_bias):
    center = jnp.mean(values, axis=-1, keepdims=True)
    centered = values - center
    inverse = lax.rsqrt(jnp.mean(centered * centered, axis=-1, keepdims=True) + EPSILON)
    normal = centered * inverse
    return (normal * norm_gain + norm_bias, normal, inverse)


def norm_back(grad_in, normal, inverse, norm_gain):
    gain_grad = jnp.sum(grad_in * normal, axis=(0, 1))
    bias_grad = jnp.sum(grad_in, axis=(0, 1))
    scaled = grad_in * norm_gain
    first = jnp.mean(scaled, axis=-1, keepdims=True)
    second = jnp.mean(scaled * normal, axis=-1, keepdims=True)
    return (inverse * (scaled - first - normal * second), gain_grad, bias_grad)


def causal_mask(length):
    row_index = lax.broadcasted_iota(jnp.int32, (length, length), 0)
    column_index = lax.broadcasted_iota(jnp.int32, (length, length), 1)
    return column_index <= row_index


def attend_forward(triple):
    queries, key_rows, value_rows = triple
    scores = jnp.einsum(
        "qhd,khd->hqk", queries, key_rows, preferred_element_type=jnp.float32
    ) * HEAD_DIM ** (-0.5)
    scores = jnp.where(causal_mask(queries.shape[0]), scores, -1e30)
    row_max = jnp.max(scores, axis=-1, keepdims=True)
    weights = jnp.exp(scores - row_max)
    totals = jnp.sum(weights, axis=-1, keepdims=True)
    shares = (weights / totals).astype(jnp.bfloat16)
    mixed = jnp.einsum("hqk,khd->qhd", shares, value_rows, preferred_element_type=jnp.float32)
    return (mixed.astype(jnp.bfloat16), row_max + jnp.log(totals))


def attend_back(group):
    queries, key_rows, value_rows, grad_mixed, log_total = group
    factor = HEAD_DIM ** (-0.5)
    scores = (
        jnp.einsum("qhd,khd->hqk", queries, key_rows, preferred_element_type=jnp.float32) * factor
    )
    scores = jnp.where(causal_mask(queries.shape[0]), scores, -1e30)
    shares = jnp.exp(scores - log_total)
    grad_value = jnp.einsum(
        "hqk,qhd->khd", shares.astype(jnp.bfloat16), grad_mixed, preferred_element_type=jnp.float32
    )
    grad_shares = jnp.einsum(
        "qhd,khd->hqk", grad_mixed, value_rows, preferred_element_type=jnp.float32
    )
    inner = jnp.sum(shares * grad_shares, axis=-1, keepdims=True)
    grad_scores = (shares * (grad_shares - inner)).astype(jnp.bfloat16)
    grad_query = (
        jnp.einsum("hqk,khd->qhd", grad_scores, key_rows, preferred_element_type=jnp.float32)
        * factor
    )
    grad_key = (
        jnp.einsum("hqk,qhd->khd", grad_scores, queries, preferred_element_type=jnp.float32)
        * factor
    )
    return jnp.stack([grad_query, grad_key, grad_value]).astype(jnp.bfloat16)


def on_device(tokens, d_out, ln1_gain, ln1_bias, w_qkv, w_out, ln2_gain, ln2_bias, w_up, w_down):
    local_rows, seq_count, width = tokens.shape
    gathered = (
        lax.all_gather(ln1_gain, "dp", axis=0, tiled=True),
        lax.all_gather(ln1_bias, "dp", axis=0, tiled=True),
        lax.all_gather(w_qkv, "dp", axis=1, tiled=True),
        lax.all_gather(w_out, "dp", axis=1, tiled=True),
        lax.all_gather(ln2_gain, "dp", axis=0, tiled=True),
        lax.all_gather(ln2_bias, "dp", axis=0, tiled=True),
        lax.all_gather(w_up, "dp", axis=0, tiled=True),
        lax.all_gather(w_down, "dp", axis=1, tiled=True),
    )
    gain_one, bias_one, qkv_weight, out_weight, gain_two, bias_two, up_weight, down_weight = (
        gathered
    )
    residual = tokens.astype(jnp.float32)
    normed_one, normal_one, inverse_one = norm_rows(
        residual, gain_one.astype(jnp.float32), bias_one.astype(jnp.float32)
    )
    low_one = normed_one.astype(jnp.bfloat16)
    rows_one = lax.all_gather(low_one, "tensor", axis=0, tiled=True)
    full_rows = rows_one.shape[0]
    projected = jnp.einsum(
        "tgd,cde->cgte", rows_one, qkv_weight, preferred_element_type=jnp.float32
    ).astype(jnp.bfloat16)
    local_width = projected.shape[3]
    heads_local = local_width // HEAD_DIM
    split_heads = projected.reshape(3, seq_count, full_rows, heads_local, HEAD_DIM)
    mixed, log_total = lax.map(attend_forward, (split_heads[0], split_heads[1], split_heads[2]))
    mixed = mixed.reshape(seq_count, full_rows, local_width)
    piece_rows = mixed
    hidden = residual + lax.psum_scatter(
        jnp.einsum(
            "gte,ed->tgd", piece_rows, out_weight, preferred_element_type=jnp.float32
        ).astype(jnp.bfloat16),
        "tensor",
        scatter_dimension=0,
        tiled=True,
    ).astype(jnp.float32)
    normed_two, normal_two, inverse_two = norm_rows(
        hidden, gain_two.astype(jnp.float32), bias_two.astype(jnp.float32)
    )
    low_two = normed_two.astype(jnp.bfloat16)
    rows_two = lax.all_gather(low_two, "tensor", axis=0, tiled=True)
    upward = jnp.einsum("tgd,df->tgf", rows_two, up_weight, preferred_element_type=jnp.float32)
    active = jax.nn.gelu(upward, approximate=True).astype(jnp.bfloat16)
    piece_rows = active
    block_sum = lax.psum_scatter(
        jnp.einsum(
            "tgf,fd->tgd", piece_rows, down_weight, preferred_element_type=jnp.float32
        ).astype(jnp.bfloat16),
        "tensor",
        scatter_dimension=0,
        tiled=True,
    ).astype(jnp.float32)
    block_out = (hidden + block_sum).astype(jnp.bfloat16)
    grad_rows = lax.all_gather(d_out, "tensor", axis=0, tiled=True)
    grad_down = jnp.einsum("tgf,tgd->fd", active, grad_rows, preferred_element_type=jnp.float32)
    grad_active = jnp.einsum(
        "tgd,fd->tgf", grad_rows, down_weight, preferred_element_type=jnp.float32
    )
    gelu_pull = jax.vjp(lambda inner: jax.nn.gelu(inner, approximate=True), upward)[1]
    grad_upward = gelu_pull(grad_active)[0].astype(jnp.bfloat16)
    grad_up = jnp.einsum("tgd,tgf->df", rows_two, grad_upward, preferred_element_type=jnp.float32)
    piece_rows = grad_upward
    grad_normed_two = lax.psum_scatter(
        jnp.einsum("tgf,df->tgd", piece_rows, up_weight, preferred_element_type=jnp.float32).astype(
            jnp.bfloat16
        ),
        "tensor",
        scatter_dimension=0,
        tiled=True,
    ).astype(jnp.float32)
    grad_hidden_norm, gain_two_grad, bias_two_grad = norm_back(
        grad_normed_two, normal_two, inverse_two, gain_two.astype(jnp.float32)
    )
    grad_hidden = d_out.astype(jnp.float32) + grad_hidden_norm
    low_hidden = grad_hidden.astype(jnp.bfloat16)
    hidden_rows = lax.all_gather(low_hidden, "tensor", axis=0, tiled=True)
    grad_out = jnp.einsum("gte,tgd->ed", mixed, hidden_rows, preferred_element_type=jnp.float32)
    grad_mixed = jnp.einsum(
        "tgd,ed->gte", hidden_rows, out_weight, preferred_element_type=jnp.float32
    ).astype(jnp.bfloat16)
    grad_heads = lax.map(
        attend_back,
        (
            split_heads[0],
            split_heads[1],
            split_heads[2],
            grad_mixed.reshape(seq_count, full_rows, heads_local, HEAD_DIM),
            log_total,
        ),
    )
    grad_projected = grad_heads.reshape(seq_count, 3, full_rows, local_width)
    grad_qkv = jnp.einsum(
        "tgd,gcte->cde", rows_one, grad_projected, preferred_element_type=jnp.float32
    )
    piece_rows = grad_projected
    grad_normed_one = lax.psum_scatter(
        jnp.einsum(
            "gcte,cde->tgd", piece_rows, qkv_weight, preferred_element_type=jnp.float32
        ).astype(jnp.bfloat16),
        "tensor",
        scatter_dimension=0,
        tiled=True,
    ).astype(jnp.float32)
    grad_input_norm, gain_one_grad, bias_one_grad = norm_back(
        grad_normed_one, normal_one, inverse_one, gain_one.astype(jnp.float32)
    )
    input_grad = (grad_hidden + grad_input_norm).astype(jnp.bfloat16)
    owned = (
        lax.psum_scatter(
            gain_one_grad.astype(jnp.bfloat16), "dp", scatter_dimension=0, tiled=True
        ).astype(jnp.float32),
        lax.psum_scatter(
            bias_one_grad.astype(jnp.bfloat16), "dp", scatter_dimension=0, tiled=True
        ).astype(jnp.float32),
        lax.psum_scatter(
            grad_qkv.astype(jnp.bfloat16), "dp", scatter_dimension=1, tiled=True
        ).astype(jnp.float32),
        lax.psum_scatter(
            grad_out.astype(jnp.bfloat16), "dp", scatter_dimension=1, tiled=True
        ).astype(jnp.float32),
        lax.psum_scatter(
            gain_two_grad.astype(jnp.bfloat16), "dp", scatter_dimension=0, tiled=True
        ).astype(jnp.float32),
        lax.psum_scatter(
            bias_two_grad.astype(jnp.bfloat16), "dp", scatter_dimension=0, tiled=True
        ).astype(jnp.float32),
        lax.psum_scatter(
            grad_up.astype(jnp.bfloat16), "dp", scatter_dimension=0, tiled=True
        ).astype(jnp.float32),
        lax.psum_scatter(
            grad_down.astype(jnp.bfloat16), "dp", scatter_dimension=1, tiled=True
        ).astype(jnp.float32),
    )
    norm_sums = lax.psum((owned[0], owned[1], owned[4], owned[5]), "tensor")
    return (
        block_out,
        input_grad,
        norm_sums[0],
        norm_sums[1],
        owned[2],
        owned[3],
        norm_sums[2],
        norm_sums[3],
        owned[6],
        owned[7],
    )


def solution(mesh):
    placed = (
        P("tensor", "dp", None),
        P("tensor", "dp", None),
        P("dp"),
        P("dp"),
        P(None, "dp", "tensor"),
        P("tensor", "dp"),
        P("dp"),
        P("dp"),
        P("dp", "tensor"),
        P("tensor", "dp"),
    )
    return jax.shard_map(
        on_device,
        mesh=mesh,
        in_specs=placed,
        out_specs=(
            P("tensor", "dp", None),
            P("tensor", "dp", None),
            P("dp"),
            P("dp"),
            P(None, "dp", "tensor"),
            P("tensor", "dp"),
            P("dp"),
            P("dp"),
            P("dp", "tensor"),
            P("tensor", "dp"),
        ),
        check_vma=False,
    )
```

profile of v0, /device:TPU:0, one launch (start us, length us, event | category | flops | bytes accessed | tf_op | source)
XLA Modules:
  0.0 1248.3 jit_solution(5901912760766693115)
XLA Ops:
  12.7 36.0 %all-reduce.11 = (bf16[1024]{0:T(1024)(128)(2,1)}, bf16[1024]{0:T(1024)(128)(2,1)}, bf16[1024]{0:T(1024)(128)(2,1)S(1)}, bf16[1024]{0:T(1024)(128)(2,1)S(1)}) all-reduce(bf16[1024]{0:T(1024)(128)(2,1)S(1)} %dynamic-update-slice.3, bf16[1024]{0:T(1024)(128)(2,1)S(1)} %dynamic-update-slice.2, ...), channel_id=1, replica_groups=mesh['dp'=16,'tensor'=2] {'dp'}, use_global_device_ids=true, to_apply=%add.3 | all-reduce | flops 4096 | bytes 16384
  57.9 52.4 %all-gather.9.cloned.1.call-done = bf16[1024,2,1024]{2,0,1:T(8,128)(2,1)} async-done(((bf16[512,2,1024]{2,0,1:T(8,128)(2,1)}), bf16[1024,2,1024]{2,0,1:T(8,128)(2,1)}) %all-gather.9.cloned.1.call-update) | async-done | bytes 4194320 | tf_op jit(solution)/shard_map/all_gather | solution.py:94
  110.3 47.4 %all-gather.11.cloned.1.call-done = bf16[3,1024,512]{2,1,0:T(8,128)(2,1)} async-done(((bf16[3,64,512]{2,1,0:T(8,128)(2,1)}), bf16[3,1024,512]{2,1,0:T(8,128)(2,1)}) %all-gather.11.cloned.1.call-update) | async-done | bytes 3145744 | tf_op jit(solution)/shard_map/all_gather | solution.py:79
  170.3 90.0 %while.22 = (s32[]{:T(128)}, bf16[2,1024,8,64]{1,3,2,0:T(8,128)(2,1)}, f32[2,8,1024,1]{2,1,3,0:T(8,128)S(1)}, bf16[2,1024,8,64]{1,3,2,0:T(8,128)(2,1)}, bf16[2,1...) while((s32[]{:T(128)}, bf16[2,1024,8,64]{1,3,2,0:T(8,128)(2,1)}, ...), condition=%wide.region_5.6_spmd, body=%wide.region_2.5_spmd.sunk | while | flops 2249711616 | bytes 117704816 | solution.py:102
  170.6 14.8 %fusion.145 = (f32[8,1024]{1,0:T(8,128)S(1)}, f32[8,1024,1024]{1,2,0:T(8,128)}) fusion(pred[1024,1024]{0,1:T(8,128)(4,1)S(1)} %iota_compare_fusion.4, bf16[2,1024,8,64]{1,3,2,0:T(8,128)(2,1)S(1)} %get-tuple-element.267, s32[]{:T(128)S(6)} %copy.93, bf16[2,1024,8,64]{1,3,2,0:T(8,128)(2,1)} %get-tuple-element.266), kind=kOutput, calls=%fused_computation.3.clone.1 | convolution fusion | flops 1098899456 | bytes 36733952 | tf_op jit(solution)/shard_map/while/body/eval_jaxpr/qhd,khd->hqk/dot_general | solution.py:35
  199.9 15.4 %fusion.147 = bf16[2,1024,8,64]{1,3,2,0:T(8,128)(2,1)} fusion(bf16[2,1024,8,64]{1,3,2,0:T(8,128)(2,1)} %get-tuple-element.256, s32[]{:T(128)S(6)} %copy.93, f32[8,1024,1024]{1,2,0:T(8,128)} %get-tuple-element.237, f32[8,1024]{1,0:T(8,128)S(1)} %fusion.146, f32[8,1024]{1,0:T(8,128)S(1)} %get-tuple-element.238, ...), kind=kOutput, calls=%fused_computation.9.clone.1 | convolution fusion | flops 1116209152 | bytes 36766720 | tf_op jit(solution)/shard_map/while/body/eval_jaxpr/hqk,khd->qhd/dot_general | solution.py:43
  215.7 14.7 %fusion.145 = (f32[8,1024]{1,0:T(8,128)S(1)}, f32[8,1024,1024]{1,2,0:T(8,128)}) fusion(pred[1024,1024]{0,1:T(8,128)(4,1)S(1)} %iota_compare_fusion.4, bf16[2,1024,8,64]{1,3,2,0:T(8,128)(2,1)S(1)} %get-tuple-element.267, s32[]{:T(128)S(6)} %copy.93, bf16[2,1024,8,64]{1,3,2,0:T(8,128)(2,1)} %get-tuple-element.266), kind=kOutput, calls=%fused_computation.3.clone.1 | convolution fusion | flops 1098899456 | bytes 36733952 | tf_op jit(solution)/shard_map/while/body/eval_jaxpr/qhd,khd->hqk/dot_general | solution.py:35
  244.8 15.4 %fusion.147 = bf16[2,1024,8,64]{1,3,2,0:T(8,128)(2,1)} fusion(bf16[2,1024,8,64]{1,3,2,0:T(8,128)(2,1)} %get-tuple-element.256, s32[]{:T(128)S(6)} %copy.93, f32[8,1024,1024]{1,2,0:T(8,128)} %get-tuple-element.237, f32[8,1024]{1,0:T(8,128)S(1)} %fusion.146, f32[8,1024]{1,0:T(8,128)S(1)} %get-tuple-element.238, ...), kind=kOutput, calls=%fused_computation.9.clone.1 | convolution fusion | flops 1116209152 | bytes 36766720 | tf_op jit(solution)/shard_map/while/body/eval_jaxpr/hqk,khd->qhd/dot_general | solution.py:43
  268.8 52.6 %reduce-scatter.8.cloned.1.call-done = bf16[512,2,1024]{2,0,1:T(8,128)(2,1)} async-done(((bf16[1024,2,1024]{2,0,1:T(8,128)(2,1)}), bf16[512,2,1024]{2,0,1:T(8,128)(2,1)}) %reduce-scatter.8.cloned.1.call-update) | async-done | bytes 2097168 | tf_op jit(solution)/shard_map/reduce_scatter | solution.py:105
  331.3 42.8 %all-gather.17.cloned.1.call-done = bf16[1024,2048]{1,0:T(8,128)(2,1)} async-done(((bf16[64,2048]{1,0:T(8,128)(2,1)}), bf16[1024,2048]{1,0:T(8,128)(2,1)}) %all-gather.17.cloned.1.call-update) | async-done | bytes 4194320 | tf_op jit(solution)/shard_map/all_gather | solution.py:83
  374.2 56.7 %all-gather.15.cloned.1.call-done = bf16[1024,2,1024]{2,0,1:T(8,128)(2,1)} async-done(((bf16[512,2,1024]{2,0,1:T(8,128)(2,1)}), bf16[1024,2,1024]{2,0,1:T(8,128)(2,1)}) %all-gather.15.cloned.1.call-update) | async-done | bytes 4194320 | tf_op jit(solution)/shard_map/all_gather | solution.py:117
  430.9 15.3 %fusion.93 = f32[1024,2,2048]{2,0,1:T(8,128)} fusion(bf16[1024,2,1024]{2,0,1:T(8,128)(2,1)} %all-gather.15.cloned.1.call-done, bf16[1024,2048]{1,0:T(8,128)(2,1)} %all-gather.17.cloned.1.call-done), kind=kOutput, calls=%fused_computation.116 | convolution fusion | flops 8589934592 | bytes 25165824 | tf_op jit(solution)/shard_map/tgd,df->tgf/dot_general | solution.py:118
  446.2 43.1 %all-gather.21.cloned.1.call-done = bf16[1024,2,1024]{2,0,1:T(8,128)(2,1)} async-done(((bf16[512,2,1024]{2,0,1:T(8,128)(2,1)}), bf16[1024,2,1024]{2,0,1:T(8,128)(2,1)}) %all-gather.21.cloned.1.call-update) | async-done | bytes 4194320 | tf_op jit(solution)/shard_map/all_gather | solution.py:130
  489.3 53.0 %all-gather.19.cloned.1.call-done = bf16[2048,1024]{0,1:T(8,128)(2,1)} async-done(((bf16[2048,64]{0,1:T(8,128)(2,1)}), bf16[2048,1024]{0,1:T(8,128)(2,1)}) %all-gather.19.cloned.1.call-update) | async-done | bytes 4194320 | tf_op jit(solution)/shard_map/all_gather | solution.py:84
  542.3 22.3 %fusion.58 = bf16[1024,2,2048]{2,0,1:T(8,128)(2,1)S(1)} fusion(f32[1024,2,2048]{2,0,1:T(8,128)} %fusion.93, bf16[1024,2,1024]{2,0,1:T(8,128)(2,1)} %all-gather.21.cloned.1.call-done, bf16[2048,1024]{0,1:T(8,128)(2,1)} %all-gather.19.cloned.1.call-done), kind=kOutput, calls=%fused_computation.68 | convolution fusion | flops 8673820672 | bytes 33554432 | tf_op jit(solution)/shard_map/tgd,fd->tgf/dot_general | solution.py:132
  578.8 52.9 %reduce-scatter.12.cloned.1.call-done = bf16[512,2,1024]{2,0,1:T(8,128)(2,1)} async-done(((bf16[1024,2,1024]{2,0,1:T(8,128)(2,1)}), bf16[512,2,1024]{2,0,1:T(8,128)(2,1)}) %reduce-scatter.12.cloned.1.call-update) | async-done | bytes 2097168 | tf_op jit(solution)/shard_map/reduce_scatter | solution.py:139
  639.5 16.0 %bitcast_convert_fusion = bf16[2048,1024]{0,1:T(8,128)(2,1)} fusion(bf16[1024,2,1024]{2,0,1:T(8,128)(2,1)} %all-gather.21.cloned.1.call-done, f32[1024,2,2048]{2,0,1:T(8,128)} %fusion.93), kind=kOutput, calls=%fused_computation.70 | convolution fusion | flops 8629780480 | bytes 25165824 | tf_op jit(solution)/shard_map/tgf,tgd->fd/dot_general | solution.py:131
  669.8 26.6 %all-gather.23.cloned.1.call-done = bf16[1024,2,1024]{2,0,1:T(8,128)(2,1)} async-done(((bf16[512,2,1024]{2,0,1:T(8,128)(2,1)}), bf16[1024,2,1024]{2,0,1:T(8,128)(2,1)}) %all-gather.23.cloned.1.call-update) | async-done | bytes 4194320 | tf_op jit(solution)/shard_map/all_gather | solution.py:152
  702.3 220.0 %while.23 = (s32[]{:T(128)}, bf16[2,3,1024,8,64]{2,4,3,1,0:T(8,128)(2,1)}, bf16[2,1024,8,64]{1,3,2,0:T(8,128)(2,1)S(1)}, bf16[2,1024,8,64]{1,3,2,0:T(8,128)(2,1)...) while((s32[]{:T(128)}, ...), condition=%wide.region_15.16_spmd, body=%wide.region_13.15_spmd.sunk | while | flops 5507637248 | bytes 272861280 | solution.py:157
  703.1 16.0 %fusion.156 = f32[8,1024,1024]{1,2,0:T(8,128)} fusion(bf16[2,1024,8,64]{1,3,2,0:T(8,128)(2,1)} %get-tuple-element.288, s32[]{:T(128)S(6)} %copy.101, bf16[2,1024,8,64]{1,3,2,0:T(8,128)(2,1)S(1)} %get-tuple-element.287), kind=kOutput, calls=%fused_computation.41.clone.1 | convolution fusion | flops 1073741824 | bytes 35652608 | tf_op jit(solution)/shard_map/while/body/eval_jaxpr/qhd,khd->hqk/dot_general | solution.py:51
  719.1 16.4 %fusion.157 = bf16[1,1,1024,8,64]{2,4,3,1,0:T(8,128)(2,1)} fusion(f32[8,1024,1024]{1,2,0:T(8,128)} %fusion.156, f32[8,1024]{1,0:T(8,128)S(1)} %dynamic-slice_bitcast_fusion.2, pred[1024,1024]{0,1:T(8,128)(4,1)S(1)} %iota_compare_fusion.5, bf16[2,1024,8,64]{1,3,2,0:T(8,128)(2,1)} %get-tuple-element.290, s32[]{:T(128)S(6)} %copy.101), kind=kOutput, calls=%fused_computation.35.clone.1 | convolution fusion | flops 1107820544 | bytes 36732932 | tf_op jit(solution)/shard_map/while/body/eval_jaxpr/hqk,qhd->khd/dot_general | solution.py:55
  735.5 24.0 %multiply_reduce_fusion.3 = (f32[8,1024]{1,0:T(8,128)S(1)}, f32[8,1024,1024]{1,2,0:T(8,128)}) fusion(f32[8,1024,1024]{1,2,0:T(8,128)} %fusion.156, f32[8,1024]{1,0:T(8,128)S(1)} %dynamic-slice_bitcast_fusion.2, pred[1024,1024]{0,1:T(8,128)(4,1)S(1)} %iota_compare_fusion.5, bf16[2,1024,8,64]{1,3,2,0:T(8,128)(2,1)} %get-tuple-element.291, ...), kind=kOutput, calls=%fused_computation.23.clone.1 | convolution fusion | flops 1115676672 | bytes 70321152 | tf_op jit(solution)/shard_map/while/body/eval_jaxpr/qhd,khd->hqk/dot_general | solution.py:58
  759.5 29.1 %multiply_convert_fusion.7 = bf16[8,1024,1024]{1,2,0:T(8,128)(2,1)} fusion(f32[8,1024,1024]{1,2,0:T(8,128)} %get-tuple-element.246, f32[8,1024,1024]{1,2,0:T(8,128)} %fusion.156, f32[8,1024]{1,0:T(8,128)S(1)} %get-tuple-element.247, f32[8,1024]{1,0:T(8,128)S(1)} %dynamic-slice_bitcast_fusion.2, pred[1024,1024]{0,1:T(8,128)(4,1)S(1)} %iota_compare_fusion.5), kind=kLoop, calls=%fused_computation.22.clone.1 | loop fusion | flops 50331648 | bytes 85000192 | tf_op jit(solution)/shard_map/while/body/eval_jaxpr/convert_element_type | solution.py:62
  829.0 16.2 %fusion.157 = bf16[1,1,1024,8,64]{2,4,3,1,0:T(8,128)(2,1)} fusion(f32[8,1024,1024]{1,2,0:T(8,128)} %fusion.156, f32[8,1024]{1,0:T(8,128)S(1)} %dynamic-slice_bitcast_fusion.2, pred[1024,1024]{0,1:T(8,128)(4,1)S(1)} %iota_compare_fusion.5, bf16[2,1024,8,64]{1,3,2,0:T(8,128)(2,1)} %get-tuple-element.290, s32[]{:T(128)S(6)} %copy.101), kind=kOutput, calls=%fused_computation.35.clone.1 | convolution fusion | flops 1107820544 | bytes 36732932 | tf_op jit(solution)/shard_map/while/body/eval_jaxpr/hqk,qhd->khd/dot_general | solution.py:55
  845.2 23.8 %multiply_reduce_fusion.3 = (f32[8,1024]{1,0:T(8,128)S(1)}, f32[8,1024,1024]{1,2,0:T(8,128)}) fusion(f32[8,1024,1024]{1,2,0:T(8,128)} %fusion.156, f32[8,1024]{1,0:T(8,128)S(1)} %dynamic-slice_bitcast_fusion.2, pred[1024,1024]{0,1:T(8,128)(4,1)S(1)} %iota_compare_fusion.5, bf16[2,1024,8,64]{1,3,2,0:T(8,128)(2,1)} %get-tuple-element.291, ...), kind=kOutput, calls=%fused_computation.23.clone.1 | convolution fusion | flops 1115676672 | bytes 70321152 | tf_op jit(solution)/shard_map/while/body/eval_jaxpr/qhd,khd->hqk/dot_general | solution.py:58
  869.0 28.5 %multiply_convert_fusion.7 = bf16[8,1024,1024]{1,2,0:T(8,128)(2,1)} fusion(f32[8,1024,1024]{1,2,0:T(8,128)} %get-tuple-element.246, f32[8,1024,1024]{1,2,0:T(8,128)} %fusion.156, f32[8,1024]{1,0:T(8,128)S(1)} %get-tuple-element.247, f32[8,1024]{1,0:T(8,128)S(1)} %dynamic-slice_bitcast_fusion.2, pred[1024,1024]{0,1:T(8,128)(4,1)S(1)} %iota_compare_fusion.5), kind=kLoop, calls=%fused_computation.22.clone.1 | loop fusion | flops 50331648 | bytes 85000192 | tf_op jit(solution)/shard_map/while/body/eval_jaxpr/convert_element_type | solution.py:62
  955.9 16.6 %fusion.104 = bf16[1024,2,1024]{2,0,1:T(8,128)(2,1)} fusion(bf16[2048,1024]{0,1:T(8,128)(2,1)} %all-gather.19.cloned.1.call-done, f32[1024,2,2048]{2,0,1:T(8,128)} %fusion.93), kind=kOutput, calls=%fused_computation.128 | convolution fusion | flops 8629780480 | bytes 25165824 | tf_op jit(solution)/shard_map/tgf,fd->tgd/dot_general | solution.py:122
  978.9 70.7 %all-reduce.14.cloned.1.call-done = bf16[3,1024,512]{2,0,1:T(4,128)(2,1)} async-done(((bf16[3,1024,512]{2,0,1:T(4,128)(2,1)}), bf16[3,1024,512]{2,0,1:T(4,128)(2,1)}) %all-reduce.14.cloned.1.call-update) | async-done | bytes 3145744
  1051.5 59.0 %reduce-scatter.16.cloned.1.call-done = bf16[512,64]{0,1:T(8,128)(2,1)} async-done(((bf16[512,1024]{0,1:T(8,128)(2,1)}), bf16[512,64]{0,1:T(8,128)(2,1)}) %reduce-scatter.16.cloned.1.call-update) | async-done | bytes 65552 | tf_op jit(solution)/shard_map/reduce_scatter | solution.py:194
  1111.9 54.0 %reduce-scatter.14.cloned.1.call-done = bf16[512,2,1024]{2,0,1:T(8,128)(2,1)} async-done(((bf16[1024,2,1024]{2,0,1:T(8,128)(2,1)}), bf16[512,2,1024]{2,0,1:T(8,128)(2,1)}) %reduce-scatter.14.cloned.1.call-update) | async-done | bytes 2097168 | tf_op jit(solution)/shard_map/reduce_scatter | solution.py:172
  1171.5 33.9 %all-reduce.10 = (bf16[1024]{0:T(1024)(128)(2,1)S(1)}, bf16[1024]{0:T(1024)(128)(2,1)S(1)}, bf16[1024]{0:T(1024)(128)(2,1)S(1)}, bf16[1024]{0:T(1024)(128)(2,1)S(1)}) all-reduce(bf16[1024]{0:T(1024)(128)(2,1)S(1)} %get-tuple-element.105, bf16[1024]{0:T(1024)(128)(2,1)S(1)} %reduce_sum.141, ...), channel_id=6, replica_groups=mesh['dp'=16,'tensor'=2] {'dp'}, use_global_device_ids=true, to_apply=%region_20.21.clone | all-reduce | flops 4096 | bytes 16384
  1205.7 16.8 %reduce-scatter.10.cloned.1.call-done = bf16[512,2,1024]{2,0,1:T(8,128)(2,1)} async-done(((bf16[1024,2,1024]{2,0,1:T(8,128)(2,1)}), bf16[512,2,1024]{2,0,1:T(8,128)(2,1)}) %reduce-scatter.10.cloned.1.call-update) | async-done | bytes 2097168 | tf_op jit(solution)/shard_map/reduce_scatter | solution.py:121
  (178 shorter events, 248.9 us)
Async XLA Ops:
  7.2 46.7 %copy-start = (bf16[512,2,1024]{2,1,0:T(2,128)(2,1)S(1)}, bf16[512,2,1024]{2,1,0:T(2,128)(2,1)}, u32[]{:S(2)}) copy-start(bf16[512,2,1024]{2,1,0:T(2,128)(2,1)} %param.14) | copy-start | bytes 6291460
  7.2 103.1 %all-gather.9.cloned.1.call-start = ((), (), s32[]{:S(2)}) async-start(), calls=%async_computation.7 | async-start | bytes 6291456 | tf_op jit(solution)/shard_map/all_gather | solution.py:94
  56.1 101.6 %all-gather.11.cloned.1.call-start = ((), (), s32[]{:S(2)}) async-start(), calls=%async_computation.8 | async-start | bytes 3342336 | tf_op jit(solution)/shard_map/all_gather | solution.py:79
  56.9 203.5 %all-gather.13.cloned.1.call-start = ((), (), s32[]{:S(2)}) async-start(), calls=%async_computation.9 | async-start | bytes 1114112 | tf_op jit(solution)/shard_map/all_gather | solution.py:80
  57.6 263.7 %reduce-scatter.8.cloned.1.call-start = ((), (), s32[]{:S(2)}) async-start(), calls=%async_computation.10 | async-start | bytes 6291456 | tf_op jit(solution)/shard_map/reduce_scatter | solution.py:105
  268.1 53.3 %copy-start.1 = (bf16[512,2,1024]{2,1,0:T(2,128)(2,1)S(1)}, bf16[512,2,1024]{2,1,0:T(2,128)(2,1)}, u32[]{:S(2)}) copy-start(bf16[512,2,1024]{2,1,0:T(2,128)(2,1)} %param.14) | copy-start | bytes 6291460
  268.1 106.1 %all-gather.17.cloned.1.call-start = ((), (), s32[]{:S(2)}) async-start(), calls=%async_computation.12 | async-start | bytes 4456448 | tf_op jit(solution)/shard_map/all_gather | solution.py:83
  268.7 162.2 %all-gather.15.cloned.1.call-start = ((), (), s32[]{:S(2)}) async-start(), calls=%async_computation.11 | async-start | bytes 6291456 | tf_op jit(solution)/shard_map/all_gather | solution.py:117
  268.8 367.8 %copy-start.12 = (f32[1024]{0:T(1024)}, f32[1024]{0:T(1024)S(1)}, u32[]{:S(2)}) copy-start(f32[1024]{0:T(1024)S(1)} %convert_element_type.162) | copy-start | bytes 12292
  323.8 312.7 %copy-start.10 = (f32[512,2]{0,1:T(2,128)}, f32[512,2]{0,1:T(2,128)S(1)}, u32[]{:S(2)}) copy-start(f32[512,2]{0,1:T(2,128)S(1)} %broadcast_multiply_fusion.4) | copy-start | bytes 12292
  324.8 311.8 %copy-start.14 = (f32[512,2]{0,1:T(2,128)}, f32[512,2]{0,1:T(2,128)S(1)}, u32[]{:S(2)}) copy-start(f32[512,2]{0,1:T(2,128)S(1)} %add_rsqrt_fusion) | copy-start | bytes 12292
  326.9 162.4 %all-gather.21.cloned.1.call-start = ((), (), s32[]{:S(2)}) async-start(), calls=%async_computation.15 | async-start | bytes 6291456 | tf_op jit(solution)/shard_map/all_gather | solution.py:130
  330.5 211.8 %all-gather.19.cloned.1.call-start = ((), (), s32[]{:S(2)}) async-start(), calls=%async_computation.13 | async-start | bytes 4456448 | tf_op jit(solution)/shard_map/all_gather | solution.py:84
  331.3 300.4 %reduce-scatter.12.cloned.1.call-start = ((), (), s32[]{:S(2)}) async-start(), calls=%async_computation.16 | async-start | bytes 6291456 | tf_op jit(solution)/shard_map/reduce_scatter | solution.py:139
  578.8 117.6 %all-gather.23.cloned.1.call-start = ((), (), s32[]{:S(2)}) async-start(), calls=%async_computation.17 | async-start | bytes 6291456 | tf_op jit(solution)/shard_map/all_gather | solution.py:152
  639.5 333.9 %reduce-scatter.20.cloned.1.call-start = ((), (), s32[]{:S(2)}) async-start(), calls=%async_computation.21 | async-start | bytes 4456448 | tf_op jit(solution)/shard_map/reduce_scatter | solution.py:206
  655.6 319.6 %reduce-scatter.18.cloned.1.call-start = ((), (), s32[]{:S(2)}) async-start(), calls=%async_computation.20 | async-start | bytes 4456448 | tf_op jit(solution)/shard_map/reduce_scatter | solution.py:203
  669.7 32.6 %copy-start.4 = (bf16[2,1024,8,64]{1,3,2,0:T(8,128)(2,1)S(1)}, bf16[2,1024,8,64]{1,3,2,0:T(8,128)(2,1)}, u32[]{:S(2)}) copy-start(bf16[2,1024,8,64]{1,3,2,0:T(8,128)(2,1)} %copy-done.3) | copy-start | bytes 6291460
  669.7 379.9 %all-reduce.14.cloned.1.call-start = ((), (), s32[]{:S(2)}) async-start(), calls=%async_computation.22 | async-start | bytes 8388608
  938.2 172.3 %reduce-scatter.16.cloned.1.call-start = ((), (), s32[]{:S(2)}) async-start(), calls=%async_computation.19 | async-start | bytes 1114112 | tf_op jit(solution)/shard_map/reduce_scatter | solution.py:194
  944.6 221.4 %reduce-scatter.14.cloned.1.call-start = ((), (), s32[]{:S(2)}) async-start(), calls=%async_computation.18 | async-start | bytes 6291456 | tf_op jit(solution)/shard_map/reduce_scatter | solution.py:172
  955.8 266.7 %reduce-scatter.10.cloned.1.call-start = ((), (), s32[]{:S(2)}) async-start(), calls=%async_computation.14 | async-start | bytes 6291456 | tf_op jit(solution)/shard_map/reduce_scatter | solution.py:121
  972.5 195.4 %copy-start.2 = (bf16[512,2,1024]{2,1,0:T(2,128)(2,1)S(1)}, bf16[512,2,1024]{2,1,0:T(2,128)(2,1)}, u32[]{:S(2)}) copy-start(bf16[512,2,1024]{2,1,0:T(2,128)(2,1)} %param.14) | copy-start | bytes 6291460
  972.5 195.4 %copy-start.17 = (f32[512,2]{0,1:T(2,128)S(1)}, f32[512,2]{0,1:T(2,128)}, u32[]{:S(2)}) copy-start(f32[512,2]{0,1:T(2,128)} %copy-done.16) | copy-start | bytes 12292
  972.5 195.4 %copy-start.19 = (f32[1024]{0:T(1024)S(1)}, f32[1024]{0:T(1024)}, u32[]{:S(2)}) copy-start(f32[1024]{0:T(1024)} %copy-done.18) | copy-start | bytes 12292
  972.5 195.4 %copy-start.21 = (f32[512,2]{0,1:T(2,128)S(1)}, f32[512,2]{0,1:T(2,128)}, u32[]{:S(2)}) copy-start(f32[512,2]{0,1:T(2,128)} %copy-done.20) | copy-start | bytes 12292
  978.9 192.6 %copy-start.26 = (bf16[1024]{0:T(1024)(128)(2,1)S(1)}, bf16[1024]{0:T(1024)(128)(2,1)}, u32[]{:S(2)}) copy-start(bf16[1024]{0:T(1024)(128)(2,1)} %get-tuple-element.103) | copy-start | bytes 6148
  978.9 243.6 %copy-start.11 = (f32[512,2]{0,1:T(2,128)S(1)}, f32[512,2]{0,1:T(2,128)}, u32[]{:S(2)}) copy-start(f32[512,2]{0,1:T(2,128)} %copy-done.10) | copy-start | bytes 12292
  978.9 243.6 %copy-start.13 = (f32[1024]{0:T(1024)S(1)}, f32[1024]{0:T(1024)}, u32[]{:S(2)}) copy-start(f32[1024]{0:T(1024)} %copy-done.12) | copy-start | bytes 12292
  978.9 243.6 %copy-start.15 = (f32[512,2]{0,1:T(2,128)S(1)}, f32[512,2]{0,1:T(2,128)}, u32[]{:S(2)}) copy-start(f32[512,2]{0,1:T(2,128)} %copy-done.14) | copy-start | bytes 12292
  978.9 243.6 %copy-start.23 = (f32[512,2]{0,1:T(2,128)S(1)}, f32[512,2]{0,1:T(2,128)}, u32[]{:S(2)}) copy-start(f32[512,2]{0,1:T(2,128)} %copy-done.22) | copy-start | bytes 12292
  978.9 243.6 %copy-start.25 = (f32[512,2]{0,1:T(2,128)S(1)}, f32[512,2]{0,1:T(2,128)}, u32[]{:S(2)}) copy-start(f32[512,2]{0,1:T(2,128)} %copy-done.24) | copy-start | bytes 12292
  (18 other events, 124.0 us)
Sparse Core Ops, SparseCore 0:
  56.3 53.9 all-gather.8
  112.5 45.2 all-gather.10
  159.9 36.7 all-gather.12
  268.2 53.0 reduce-scatter.7
  323.6 50.5 all-gather.16
  375.6 55.2 all-gather.14
  432.5 56.7 all-gather.20
  491.7 50.5 all-gather.18
  578.9 52.7 reduce-scatter.11
  639.6 56.7 all-gather.22
  700.3 72.4 reduce-scatter.19
  777.0 71.4 reduce-scatter.17
  938.3 111.2 all-reduce.13
  1054.1 56.2 reduce-scatter.15
  1112.6 53.3 reduce-scatter.13
  1168.2 54.2 reduce-scatter.9
where the time goes:
time: 1250 us
  waiting for transfers between devices  631 us (50%)
  matrix products  359 us (29%)
  other arithmetic  135 us (11%)
  blocking collectives  75.3 us (6%)
  local copies, waits for them, and re-layouts  30.2 us (2%)
  between operations  16.1 us (1%)
    unnamed x17, waiting for transfers between devices  73.5 us
    unnamed x2, blocking collectives  69.9 us
    reduce_scatter x1, waiting for transfers between devices, on_device(): lax.psum_scatter(grad_out.astype(jnp.bfloat16), 'dp', scatter_dimension=1...  59 us
    convert_element_type x2, other arithmetic, attend_back(): grad_scores = (shares * (grad_shares - inner)).astype(jnp.bfloat16)  57.6 us
    all_gather x1, waiting for transfers between devices, on_device(): rows_two = lax.all_gather(low_two, 'tensor', axis=0, tiled=True)  56.7 us
    reduce_scatter x1, waiting for transfers between devices, on_device(): lax.psum_scatter(jnp.einsum('gcte,cde->tgd', piece_rows, qkv_weight, pref...  54 us
    all_gather x1, waiting for transfers between devices, on_device(): lax.all_gather(w_down, 'dp', axis=1, tiled=True)  53 us
    reduce_scatter x1, waiting for transfers between devices, on_device(): lax.psum_scatter(jnp.einsum('tgf,df->tgd', piece_rows, up_weight, preferr...  52.9 us
  transfers between devices with their start and end apart: 16, of which 13 were waited for; matrix products, arithmetic and copies ran while one was open for 36% of the time, Pallas kernels for 0%

commit v1 on v0

--- a/solution.py
+++ b/solution.py
@@ -127,7 +127,26 @@
         tiled=True,
     ).astype(jnp.float32)
     block_out = (hidden + block_sum).astype(jnp.bfloat16)
-    grad_rows = lax.all_gather(d_out, "tensor", axis=0, tiled=True)
+    after, shaped, reached = (
+        jax.lax.axis_size("tensor"),
+        jax.lax.axis_index("tensor"),
+        d_out.shape[0],
+    )
+    piece_out, carry_in = (d_out, 1)
+    while carry_in < after:
+        piece_out = jnp.concatenate(
+            [
+                piece_out,
+                jax.lax.ppermute(
+                    piece_out,
+                    "tensor",
+                    tuple(((kk, (kk - carry_in) % after) for kk in range(after))),
+                ),
+            ],
+            0,
+        )
+        carry_in = 2 * carry_in
+    grad_rows = jnp.roll(piece_out, shaped * reached, 0)
     grad_down = jnp.einsum("tgf,tgd->fd", active, grad_rows, preferred_element_type=jnp.float32)
     grad_active = jnp.einsum(
         "tgd,fd->tgf", grad_rows, down_weight, preferred_element_type=jnp.float32

time: 1250 us -> 1190 us (0.952)
  waiting for transfers between devices: 631 us -> 564 us
    ppermute x0 -> x1, waiting for transfers between devices: none -> 47.4 us  [on_device(): jax.lax.ppermute(piece_out, 'tensor', tuple(((kk, (kk - carry_in) % after...]
    all_gather x1 -> x0, waiting for transfers between devices: 43.1 us -> none  [on_device(): grad_rows = lax.all_gather(d_out, 'tensor', axis=0, tiled=True)]
    all_gather x1, waiting for transfers between devices: 42.8 us -> 0.01 us  [on_device(): lax.all_gather(w_up, 'dp', axis=0, tiled=True)]
    all_gather x1, waiting for transfers between devices: 53 us -> 37.7 us  [on_device(): lax.all_gather(w_down, 'dp', axis=1, tiled=True)]
    all_gather x1, waiting for transfers between devices: 56.7 us -> 43.9 us  [on_device(): rows_two = lax.all_gather(low_two, 'tensor', axis=0, tiled=True)]
    unnamed x17 -> x16, waiting for transfers between devices: 73.5 us -> 73.2 us
  transfers between devices with their start and end apart: 16 -> 16, of which waited for: 13 -> 12; matrix products, arithmetic and copies ran while one was open for 36% -> 38% of each run, Pallas kernels for 0% -> 0%
where the time goes in v1:
time: 1190 us
  waiting for transfers between devices  564 us (47%)
  matrix products  359 us (30%)
  other arithmetic  144 us (12%)
  blocking collectives  75.2 us (6%)
  local copies, waits for them, and re-layouts  30.1 us (3%)
  between operations  16 us (1%)
    unnamed x16, waiting for transfers between devices  73.2 us
    unnamed x2, blocking collectives  69.8 us
    reduce_scatter x1, waiting for transfers between devices, on_device(): lax.psum_scatter(grad_out.astype(jnp.bfloat16), 'dp', scatter_dimension=1...  59.1 us
    convert_element_type x2, other arithmetic, attend_back(): grad_scores = (shares * (grad_shares - inner)).astype(jnp.bfloat16)  57.5 us
    reduce_scatter x1, waiting for transfers between devices, on_device(): lax.psum_scatter(jnp.einsum('gcte,cde->tgd', piece_rows, qkv_weight, pref...  54 us
    reduce_scatter x1, waiting for transfers between devices, on_device(): lax.psum_scatter(jnp.einsum('tgf,df->tgd', piece_rows, up_weight, preferr...  52.9 us
    reduce_scatter x1, waiting for transfers between devices, on_device(): lax.psum_scatter(jnp.einsum('gte,ed->tgd', piece_rows, out_weight, prefer...  52.6 us
    all_gather x1, waiting for transfers between devices, on_device(): rows_one = lax.all_gather(low_one, 'tensor', axis=0, tiled=True)  52.3 us
  transfers between devices with their start and end apart: 16, of which 12 were waited for; matrix products, arithmetic and copies ran while one was open for 38% of the time, Pallas kernels for 0%

profile of v1, /device:TPU:0, one launch (start us, length us, event | category | flops | bytes accessed | tf_op | source)
XLA Modules:
  0.0 1190.3 jit_solution(13021504561515831622)
XLA Ops:
  12.7 36.0 %all-reduce.11 = (bf16[1024]{0:T(1024)(128)(2,1)}, bf16[1024]{0:T(1024)(128)(2,1)}, bf16[1024]{0:T(1024)(128)(2,1)S(1)}, bf16[1024]{0:T(1024)(128)(2,1)S(1)}) all-reduce(bf16[1024]{0:T(1024)(128)(2,1)S(1)} %dynamic-update-slice.3, bf16[1024]{0:T(1024)(128)(2,1)S(1)} %dynamic-update-slice.2, ...), channel_id=1, replica_groups=mesh['dp'=16,'tensor'=2] {'dp'}, use_global_device_ids=true, to_apply=%add.3 | all-reduce | flops 4096 | bytes 16384
  58.0 52.3 %all-gather.8.cloned.1.call-done = bf16[1024,2,1024]{2,0,1:T(8,128)(2,1)} async-done(((bf16[512,2,1024]{2,0,1:T(8,128)(2,1)}), bf16[1024,2,1024]{2,0,1:T(8,128)(2,1)}) %all-gather.8.cloned.1.call-update) | async-done | bytes 4194320 | tf_op jit(solution)/shard_map/all_gather | solution.py:94
  110.3 47.4 %all-gather.10.cloned.1.call-done = bf16[3,1024,512]{2,1,0:T(8,128)(2,1)} async-done(((bf16[3,64,512]{2,1,0:T(8,128)(2,1)}), bf16[3,1024,512]{2,1,0:T(8,128)(2,1)}) %all-gather.10.cloned.1.call-update) | async-done | bytes 3145744 | tf_op jit(solution)/shard_map/all_gather | solution.py:79
  170.4 90.4 %while.22 = (s32[]{:T(128)}, bf16[2,1024,8,64]{1,3,2,0:T(8,128)(2,1)}, f32[2,8,1024,1]{2,1,3,0:T(8,128)S(1)}, bf16[2,1024,8,64]{1,3,2,0:T(8,128)(2,1)}, bf16[2,1...) while((s32[]{:T(128)}, bf16[2,1024,8,64]{1,3,2,0:T(8,128)(2,1)}, ...), condition=%wide.region_5.6_spmd, body=%wide.region_2.5_spmd.sunk | while | flops 2249711616 | bytes 117704816 | solution.py:102
  170.7 14.9 %fusion.148 = (f32[8,1024]{1,0:T(8,128)S(1)}, f32[8,1024,1024]{1,2,0:T(8,128)}) fusion(pred[1024,1024]{0,1:T(8,128)(4,1)S(1)} %iota_compare_fusion.4, bf16[2,1024,8,64]{1,3,2,0:T(8,128)(2,1)S(1)} %get-tuple-element.267, s32[]{:T(128)S(6)} %copy.97, bf16[2,1024,8,64]{1,3,2,0:T(8,128)(2,1)} %get-tuple-element.266), kind=kOutput, calls=%fused_computation.3.clone.1 | convolution fusion | flops 1098899456 | bytes 36733952 | tf_op jit(solution)/shard_map/while/body/eval_jaxpr/qhd,khd->hqk/dot_general | solution.py:35
  200.0 15.4 %fusion.150 = bf16[2,1024,8,64]{1,3,2,0:T(8,128)(2,1)} fusion(bf16[2,1024,8,64]{1,3,2,0:T(8,128)(2,1)} %get-tuple-element.256, s32[]{:T(128)S(6)} %copy.97, f32[8,1024,1024]{1,2,0:T(8,128)} %get-tuple-element.237, f32[8,1024]{1,0:T(8,128)S(1)} %fusion.149, f32[8,1024]{1,0:T(8,128)S(1)} %get-tuple-element.238, ...), kind=kOutput, calls=%fused_computation.9.clone.1 | convolution fusion | flops 1116209152 | bytes 36766720 | tf_op jit(solution)/shard_map/while/body/eval_jaxpr/hqk,khd->qhd/dot_general | solution.py:43
  215.7 14.7 %fusion.148 = (f32[8,1024]{1,0:T(8,128)S(1)}, f32[8,1024,1024]{1,2,0:T(8,128)}) fusion(pred[1024,1024]{0,1:T(8,128)(4,1)S(1)} %iota_compare_fusion.4, bf16[2,1024,8,64]{1,3,2,0:T(8,128)(2,1)S(1)} %get-tuple-element.267, s32[]{:T(128)S(6)} %copy.97, bf16[2,1024,8,64]{1,3,2,0:T(8,128)(2,1)} %get-tuple-element.266), kind=kOutput, calls=%fused_computation.3.clone.1 | convolution fusion | flops 1098899456 | bytes 36733952 | tf_op jit(solution)/shard_map/while/body/eval_jaxpr/qhd,khd->hqk/dot_general | solution.py:35
  244.8 15.4 %fusion.150 = bf16[2,1024,8,64]{1,3,2,0:T(8,128)(2,1)} fusion(bf16[2,1024,8,64]{1,3,2,0:T(8,128)(2,1)} %get-tuple-element.256, s32[]{:T(128)S(6)} %copy.97, f32[8,1024,1024]{1,2,0:T(8,128)} %get-tuple-element.237, f32[8,1024]{1,0:T(8,128)S(1)} %fusion.149, f32[8,1024]{1,0:T(8,128)S(1)} %get-tuple-element.238, ...), kind=kOutput, calls=%fused_computation.9.clone.1 | convolution fusion | flops 1116209152 | bytes 36766720 | tf_op jit(solution)/shard_map/while/body/eval_jaxpr/hqk,khd->qhd/dot_general | solution.py:43
  269.1 52.6 %reduce-scatter.8.cloned.1.call-done = bf16[512,2,1024]{2,0,1:T(8,128)(2,1)} async-done(((bf16[1024,2,1024]{2,0,1:T(8,128)(2,1)}), bf16[512,2,1024]{2,0,1:T(8,128)(2,1)}) %reduce-scatter.8.cloned.1.call-update) | async-done | bytes 2097168 | tf_op jit(solution)/shard_map/reduce_scatter | solution.py:105
  331.8 47.4 %collective-permute-done = bf16[512,2,1024]{2,0,1:T(8,128)(2,1)} collective-permute-done((bf16[512,2,1024]{2,0,1:T(8,128)(2,1)}, bf16[512,2,1024]{2,0,1:T(8,128)(2,1)}, u32[]{:S(2)}, u32[]{:S(2)}) %collective-permute-start) | collective-permute-done | bytes 2097184 | tf_op jit(solution)/shard_map/ppermute | solution.py:140
  387.5 43.9 %all-gather.14.cloned.1.call-done = bf16[1024,2,1024]{2,0,1:T(8,128)(2,1)} async-done(((bf16[512,2,1024]{2,0,1:T(8,128)(2,1)}), bf16[1024,2,1024]{2,0,1:T(8,128)(2,1)}) %all-gather.14.cloned.1.call-update) | async-done | bytes 4194320 | tf_op jit(solution)/shard_map/all_gather | solution.py:117
  431.4 15.3 %fusion.96 = f32[1024,2,2048]{2,0,1:T(8,128)} fusion(bf16[1024,2,1024]{2,0,1:T(8,128)(2,1)} %all-gather.14.cloned.1.call-done, bf16[1024,2048]{1,0:T(8,128)(2,1)} %all-gather.16.cloned.1.call-done), kind=kOutput, calls=%fused_computation.123 | convolution fusion | flops 8589934592 | bytes 25165824 | tf_op jit(solution)/shard_map/tgd,df->tgf/dot_general | solution.py:118
  446.7 37.7 %all-gather.18.cloned.1.call-done = bf16[2048,1024]{0,1:T(8,128)(2,1)} async-done(((bf16[2048,64]{0,1:T(8,128)(2,1)}), bf16[2048,1024]{0,1:T(8,128)(2,1)}) %all-gather.18.cloned.1.call-update) | async-done | bytes 4194320 | tf_op jit(solution)/shard_map/all_gather | solution.py:84
  484.4 22.4 %fusion.58 = bf16[1024,2,2048]{2,0,1:T(8,128)(2,1)S(1)} fusion(f32[1024,2,2048]{2,0,1:T(8,128)} %fusion.96, bf16[1024,2,1024]{2,0,1:T(8,128)(2,1)} %fusion.86, bf16[2048,1024]{0,1:T(8,128)(2,1)} %all-gather.18.cloned.1.call-done), kind=kOutput, calls=%fused_computation.68 | convolution fusion | flops 8673820672 | bytes 33554432 | tf_op jit(solution)/shard_map/tgd,fd->tgf/dot_general | solution.py:151
  520.6 52.9 %reduce-scatter.12.cloned.1.call-done = bf16[512,2,1024]{2,0,1:T(8,128)(2,1)} async-done(((bf16[1024,2,1024]{2,0,1:T(8,128)(2,1)}), bf16[512,2,1024]{2,0,1:T(8,128)(2,1)}) %reduce-scatter.12.cloned.1.call-update) | async-done | bytes 2097168 | tf_op jit(solution)/shard_map/reduce_scatter | solution.py:158
  581.8 15.8 %bitcast_convert_fusion = bf16[2048,1024]{0,1:T(8,128)(2,1)} fusion(bf16[1024,2,1024]{2,0,1:T(8,128)(2,1)} %fusion.86, f32[1024,2,2048]{2,0,1:T(8,128)} %fusion.96), kind=kOutput, calls=%fused_computation.74 | convolution fusion | flops 8629780480 | bytes 25165824 | tf_op jit(solution)/shard_map/tgf,tgd->fd/dot_general | solution.py:150
  611.9 26.8 %all-gather.20.cloned.1.call-done = bf16[1024,2,1024]{2,0,1:T(8,128)(2,1)} async-done(((bf16[512,2,1024]{2,0,1:T(8,128)(2,1)}), bf16[1024,2,1024]{2,0,1:T(8,128)(2,1)}) %all-gather.20.cloned.1.call-update) | async-done | bytes 4194320 | tf_op jit(solution)/shard_map/all_gather | solution.py:171
  644.6 219.7 %while.23 = (s32[]{:T(128)}, bf16[2,3,1024,8,64]{2,4,3,1,0:T(8,128)(2,1)}, bf16[2,1024,8,64]{1,3,2,0:T(8,128)(2,1)S(1)}, bf16[2,1024,8,64]{1,3,2,0:T(8,128)(2,1)...) while((s32[]{:T(128)}, ...), condition=%wide.region_15.16_spmd, body=%wide.region_13.15_spmd.sunk | while | flops 5507637248 | bytes 272861280 | solution.py:176
  645.1 16.1 %fusion.159 = f32[8,1024,1024]{1,2,0:T(8,128)} fusion(bf16[2,1024,8,64]{1,3,2,0:T(8,128)(2,1)} %get-tuple-element.288, s32[]{:T(128)S(6)} %copy.105, bf16[2,1024,8,64]{1,3,2,0:T(8,128)(2,1)S(1)} %get-tuple-element.287), kind=kOutput, calls=%fused_computation.41.clone.1 | convolution fusion | flops 1073741824 | bytes 35652608 | tf_op jit(solution)/shard_map/while/body/eval_jaxpr/qhd,khd->hqk/dot_general | solution.py:51
  661.2 16.3 %fusion.160 = bf16[1,1,1024,8,64]{2,4,3,1,0:T(8,128)(2,1)} fusion(f32[8,1024,1024]{1,2,0:T(8,128)} %fusion.159, f32[8,1024]{1,0:T(8,128)S(1)} %dynamic-slice_bitcast_fusion.2, pred[1024,1024]{0,1:T(8,128)(4,1)S(1)} %iota_compare_fusion.5, bf16[2,1024,8,64]{1,3,2,0:T(8,128)(2,1)} %get-tuple-element.290, s32[]{:T(128)S(6)} %copy.105), kind=kOutput, calls=%fused_computation.35.clone.1 | convolution fusion | flops 1107820544 | bytes 36732932 | tf_op jit(solution)/shard_map/while/body/eval_jaxpr/hqk,qhd->khd/dot_general | solution.py:55
  677.5 24.0 %multiply_reduce_fusion.3 = (f32[8,1024]{1,0:T(8,128)S(1)}, f32[8,1024,1024]{1,2,0:T(8,128)}) fusion(f32[8,1024,1024]{1,2,0:T(8,128)} %fusion.159, f32[8,1024]{1,0:T(8,128)S(1)} %dynamic-slice_bitcast_fusion.2, pred[1024,1024]{0,1:T(8,128)(4,1)S(1)} %iota_compare_fusion.5, bf16[2,1024,8,64]{1,3,2,0:T(8,128)(2,1)} %get-tuple-element.291, ...), kind=kOutput, calls=%fused_computation.23.clone.1 | convolution fusion | flops 1115676672 | bytes 70321152 | tf_op jit(solution)/shard_map/while/body/eval_jaxpr/qhd,khd->hqk/dot_general | solution.py:58
  701.5 29.0 %multiply_convert_fusion.7 = bf16[8,1024,1024]{1,2,0:T(8,128)(2,1)} fusion(f32[8,1024,1024]{1,2,0:T(8,128)} %get-tuple-element.246, f32[8,1024,1024]{1,2,0:T(8,128)} %fusion.159, f32[8,1024]{1,0:T(8,128)S(1)} %get-tuple-element.247, f32[8,1024]{1,0:T(8,128)S(1)} %dynamic-slice_bitcast_fusion.2, pred[1024,1024]{0,1:T(8,128)(4,1)S(1)} %iota_compare_fusion.5), kind=kLoop, calls=%fused_computation.22.clone.1 | loop fusion | flops 50331648 | bytes 85000192 | tf_op jit(solution)/shard_map/while/body/eval_jaxpr/convert_element_type | solution.py:62
  756.4 14.6 %fusion.159 = f32[8,1024,1024]{1,2,0:T(8,128)} fusion(bf16[2,1024,8,64]{1,3,2,0:T(8,128)(2,1)} %get-tuple-element.288, s32[]{:T(128)S(6)} %copy.105, bf16[2,1024,8,64]{1,3,2,0:T(8,128)(2,1)S(1)} %get-tuple-element.287), kind=kOutput, calls=%fused_computation.41.clone.1 | convolution fusion | flops 1073741824 | bytes 35652608 | tf_op jit(solution)/shard_map/while/body/eval_jaxpr/qhd,khd->hqk/dot_general | solution.py:51
  771.0 16.2 %fusion.160 = bf16[1,1,1024,8,64]{2,4,3,1,0:T(8,128)(2,1)} fusion(f32[8,1024,1024]{1,2,0:T(8,128)} %fusion.159, f32[8,1024]{1,0:T(8,128)S(1)} %dynamic-slice_bitcast_fusion.2, pred[1024,1024]{0,1:T(8,128)(4,1)S(1)} %iota_compare_fusion.5, bf16[2,1024,8,64]{1,3,2,0:T(8,128)(2,1)} %get-tuple-element.290, s32[]{:T(128)S(6)} %copy.105), kind=kOutput, calls=%fused_computation.35.clone.1 | convolution fusion | flops 1107820544 | bytes 36732932 | tf_op jit(solution)/shard_map/while/body/eval_jaxpr/hqk,qhd->khd/dot_general | solution.py:55
  787.1 23.8 %multiply_reduce_fusion.3 = (f32[8,1024]{1,0:T(8,128)S(1)}, f32[8,1024,1024]{1,2,0:T(8,128)}) fusion(f32[8,1024,1024]{1,2,0:T(8,128)} %fusion.159, f32[8,1024]{1,0:T(8,128)S(1)} %dynamic-slice_bitcast_fusion.2, pred[1024,1024]{0,1:T(8,128)(4,1)S(1)} %iota_compare_fusion.5, bf16[2,1024,8,64]{1,3,2,0:T(8,128)(2,1)} %get-tuple-element.291, ...), kind=kOutput, calls=%fused_computation.23.clone.1 | convolution fusion | flops 1115676672 | bytes 70321152 | tf_op jit(solution)/shard_map/while/body/eval_jaxpr/qhd,khd->hqk/dot_general | solution.py:58
  810.9 28.5 %multiply_convert_fusion.7 = bf16[8,1024,1024]{1,2,0:T(8,128)(2,1)} fusion(f32[8,1024,1024]{1,2,0:T(8,128)} %get-tuple-element.246, f32[8,1024,1024]{1,2,0:T(8,128)} %fusion.159, f32[8,1024]{1,0:T(8,128)S(1)} %get-tuple-element.247, f32[8,1024]{1,0:T(8,128)S(1)} %dynamic-slice_bitcast_fusion.2, pred[1024,1024]{0,1:T(8,128)(4,1)S(1)} %iota_compare_fusion.5), kind=kLoop, calls=%fused_computation.22.clone.1 | loop fusion | flops 50331648 | bytes 85000192 | tf_op jit(solution)/shard_map/while/body/eval_jaxpr/convert_element_type | solution.py:62
  897.9 16.8 %fusion.107 = bf16[1024,2,1024]{2,0,1:T(8,128)(2,1)} fusion(bf16[2048,1024]{0,1:T(8,128)(2,1)} %all-gather.18.cloned.1.call-done, f32[1024,2,2048]{2,0,1:T(8,128)} %fusion.96), kind=kOutput, calls=%fused_computation.135 | convolution fusion | flops 8629780480 | bytes 25165824 | tf_op jit(solution)/shard_map/tgf,fd->tgd/dot_general | solution.py:122
  921.2 70.4 %all-reduce.14.cloned.1.call-done = bf16[3,1024,512]{2,0,1:T(4,128)(2,1)} async-done(((bf16[3,1024,512]{2,0,1:T(4,128)(2,1)}), bf16[3,1024,512]{2,0,1:T(4,128)(2,1)}) %all-reduce.14.cloned.1.call-update) | async-done | bytes 3145744
  993.5 59.1 %reduce-scatter.16.cloned.1.call-done = bf16[512,64]{0,1:T(8,128)(2,1)} async-done(((bf16[512,1024]{0,1:T(8,128)(2,1)}), bf16[512,64]{0,1:T(8,128)(2,1)}) %reduce-scatter.16.cloned.1.call-update) | async-done | bytes 65552 | tf_op jit(solution)/shard_map/reduce_scatter | solution.py:213
  1054.1 54.0 %reduce-scatter.14.cloned.1.call-done = bf16[512,2,1024]{2,0,1:T(8,128)(2,1)} async-done(((bf16[1024,2,1024]{2,0,1:T(8,128)(2,1)}), bf16[512,2,1024]{2,0,1:T(8,128)(2,1)}) %reduce-scatter.14.cloned.1.call-update) | async-done | bytes 2097168 | tf_op jit(solution)/shard_map/reduce_scatter | solution.py:191
  1113.6 33.8 %all-reduce.10 = (bf16[1024]{0:T(1024)(128)(2,1)S(1)}, bf16[1024]{0:T(1024)(128)(2,1)S(1)}, bf16[1024]{0:T(1024)(128)(2,1)S(1)}, bf16[1024]{0:T(1024)(128)(2,1)S(1)}) all-reduce(bf16[1024]{0:T(1024)(128)(2,1)S(1)} %get-tuple-element.105, bf16[1024]{0:T(1024)(128)(2,1)S(1)} %reduce_sum.141, ...), channel_id=6, replica_groups=mesh['dp'=16,'tensor'=2] {'dp'}, use_global_device_ids=true, to_apply=%region_20.21.clone | all-reduce | flops 4096 | bytes 16384
  1147.8 16.9 %reduce-scatter.10.cloned.1.call-done = bf16[512,2,1024]{2,0,1:T(8,128)(2,1)} async-done(((bf16[1024,2,1024]{2,0,1:T(8,128)(2,1)}), bf16[512,2,1024]{2,0,1:T(8,128)(2,1)}) %reduce-scatter.10.cloned.1.call-update) | async-done | bytes 2097168 | tf_op jit(solution)/shard_map/reduce_scatter | solution.py:121
  (178 shorter events, 242.9 us)
Async XLA Ops:
  7.2 46.8 %copy-start = (bf16[512,2,1024]{2,1,0:T(2,128)(2,1)S(1)}, bf16[512,2,1024]{2,1,0:T(2,128)(2,1)}, u32[]{:S(2)}) copy-start(bf16[512,2,1024]{2,1,0:T(2,128)(2,1)} %param.14) | copy-start | bytes 6291460
  7.2 103.1 %all-gather.8.cloned.1.call-start = ((), (), s32[]{:S(2)}) async-start(), calls=%async_computation.7 | async-start | bytes 6291456 | tf_op jit(solution)/shard_map/all_gather | solution.py:94
  56.2 101.6 %all-gather.10.cloned.1.call-start = ((), (), s32[]{:S(2)}) async-start(), calls=%async_computation.8 | async-start | bytes 3342336 | tf_op jit(solution)/shard_map/all_gather | solution.py:79
  56.9 203.9 %all-gather.12.cloned.1.call-start = ((), (), s32[]{:S(2)}) async-start(), calls=%async_computation.9 | async-start | bytes 1114112 | tf_op jit(solution)/shard_map/all_gather | solution.py:80
  57.6 264.0 %reduce-scatter.8.cloned.1.call-start = ((), (), s32[]{:S(2)}) async-start(), calls=%async_computation.10 | async-start | bytes 6291456 | tf_op jit(solution)/shard_map/reduce_scatter | solution.py:105
  268.4 53.3 %copy-start.1 = (bf16[512,2,1024]{2,1,0:T(2,128)(2,1)S(1)}, bf16[512,2,1024]{2,1,0:T(2,128)(2,1)}, u32[]{:S(2)}) copy-start(bf16[512,2,1024]{2,1,0:T(2,128)(2,1)} %param.14) | copy-start | bytes 6291460
  268.4 119.1 %all-gather.16.cloned.1.call-start = ((), (), s32[]{:S(2)}) async-start(), calls=%async_computation.12 | async-start | bytes 4456448 | tf_op jit(solution)/shard_map/all_gather | solution.py:83
  269.0 162.4 %all-gather.14.cloned.1.call-start = ((), (), s32[]{:S(2)}) async-start(), calls=%async_computation.11 | async-start | bytes 6291456 | tf_op jit(solution)/shard_map/all_gather | solution.py:117
  269.1 309.7 %copy-start.12 = (f32[1024]{0:T(1024)}, f32[1024]{0:T(1024)S(1)}, u32[]{:S(2)}) copy-start(f32[1024]{0:T(1024)S(1)} %convert_element_type.162) | copy-start | bytes 12292
  324.1 254.7 %copy-start.10 = (f32[512,2]{0,1:T(2,128)}, f32[512,2]{0,1:T(2,128)S(1)}, u32[]{:S(2)}) copy-start(f32[512,2]{0,1:T(2,128)S(1)} %broadcast_multiply_fusion.4) | copy-start | bytes 12292
  325.1 253.7 %copy-start.14 = (f32[512,2]{0,1:T(2,128)}, f32[512,2]{0,1:T(2,128)S(1)}, u32[]{:S(2)}) copy-start(f32[512,2]{0,1:T(2,128)S(1)} %add_rsqrt_fusion) | copy-start | bytes 12292
  327.1 157.2 %all-gather.18.cloned.1.call-start = ((), (), s32[]{:S(2)}) async-start(), calls=%async_computation.13 | async-start | bytes 4456448 | tf_op jit(solution)/shard_map/all_gather | solution.py:84
  327.9 245.6 %reduce-scatter.12.cloned.1.call-start = ((), (), s32[]{:S(2)}) async-start(), calls=%async_computation.15 | async-start | bytes 6291456 | tf_op jit(solution)/shard_map/reduce_scatter | solution.py:158
  331.5 47.7 %collective-permute-start = (bf16[512,2,1024]{2,0,1:T(8,128)(2,1)}, bf16[512,2,1024]{2,0,1:T(8,128)(2,1)}, u32[]{:S(2)}, u32[]{:S(2)}) collective-permute-start(bf16[512,2,1024]{2,0,1:T(8,128)(2,1)} %copy.45), channel_id=1, source_target_pairs={{0,1},{1,0},{2,3},{3,2},{4,5},{5,4},{6,7},{7,6},{8,9},{9,8},{10,11... | collective-permute-start | bytes 6291464 | tf_op jit(solution)/shard_map/ppermute | solution.py:140
  520.6 118.1 %all-gather.20.cloned.1.call-start = ((), (), s32[]{:S(2)}) async-start(), calls=%async_computation.16 | async-start | bytes 6291456 | tf_op jit(solution)/shard_map/all_gather | solution.py:171
  581.8 333.8 %reduce-scatter.20.cloned.1.call-start = ((), (), s32[]{:S(2)}) async-start(), calls=%async_computation.20 | async-start | bytes 4456448 | tf_op jit(solution)/shard_map/reduce_scatter | solution.py:225
  597.7 319.7 %reduce-scatter.18.cloned.1.call-start = ((), (), s32[]{:S(2)}) async-start(), calls=%async_computation.19 | async-start | bytes 4456448 | tf_op jit(solution)/shard_map/reduce_scatter | solution.py:222
  611.8 32.8 %copy-start.4 = (bf16[2,1024,8,64]{1,3,2,0:T(8,128)(2,1)S(1)}, bf16[2,1024,8,64]{1,3,2,0:T(8,128)(2,1)}, u32[]{:S(2)}) copy-start(bf16[2,1024,8,64]{1,3,2,0:T(8,128)(2,1)} %copy-done.3) | copy-start | bytes 6291460
  611.8 379.8 %all-reduce.14.cloned.1.call-start = ((), (), s32[]{:S(2)}) async-start(), calls=%async_computation.21 | async-start | bytes 8388608
  880.2 172.4 %reduce-scatter.16.cloned.1.call-start = ((), (), s32[]{:S(2)}) async-start(), calls=%async_computation.18 | async-start | bytes 1114112 | tf_op jit(solution)/shard_map/reduce_scatter | solution.py:213
  886.6 221.5 %reduce-scatter.14.cloned.1.call-start = ((), (), s32[]{:S(2)}) async-start(), calls=%async_computation.17 | async-start | bytes 6291456 | tf_op jit(solution)/shard_map/reduce_scatter | solution.py:191
  897.9 266.8 %reduce-scatter.10.cloned.1.call-start = ((), (), s32[]{:S(2)}) async-start(), calls=%async_computation.14 | async-start | bytes 6291456 | tf_op jit(solution)/shard_map/reduce_scatter | solution.py:121
  914.7 195.3 %copy-start.2 = (bf16[512,2,1024]{2,1,0:T(2,128)(2,1)S(1)}, bf16[512,2,1024]{2,1,0:T(2,128)(2,1)}, u32[]{:S(2)}) copy-start(bf16[512,2,1024]{2,1,0:T(2,128)(2,1)} %param.14) | copy-start | bytes 6291460
  914.8 195.3 %copy-start.17 = (f32[512,2]{0,1:T(2,128)S(1)}, f32[512,2]{0,1:T(2,128)}, u32[]{:S(2)}) copy-start(f32[512,2]{0,1:T(2,128)} %copy-done.16) | copy-start | bytes 12292
  914.8 195.3 %copy-start.19 = (f32[1024]{0:T(1024)S(1)}, f32[1024]{0:T(1024)}, u32[]{:S(2)}) copy-start(f32[1024]{0:T(1024)} %copy-done.18) | copy-start | bytes 12292
  914.8 195.3 %copy-start.21 = (f32[512,2]{0,1:T(2,128)S(1)}, f32[512,2]{0,1:T(2,128)}, u32[]{:S(2)}) copy-start(f32[512,2]{0,1:T(2,128)} %copy-done.20) | copy-start | bytes 12292
  921.1 192.5 %copy-start.26 = (bf16[1024]{0:T(1024)(128)(2,1)S(1)}, bf16[1024]{0:T(1024)(128)(2,1)}, u32[]{:S(2)}) copy-start(bf16[1024]{0:T(1024)(128)(2,1)} %get-tuple-element.103) | copy-start | bytes 6148
  921.1 243.5 %copy-start.11 = (f32[512,2]{0,1:T(2,128)S(1)}, f32[512,2]{0,1:T(2,128)}, u32[]{:S(2)}) copy-start(f32[512,2]{0,1:T(2,128)} %copy-done.10) | copy-start | bytes 12292
  921.1 243.5 %copy-start.13 = (f32[1024]{0:T(1024)S(1)}, f32[1024]{0:T(1024)}, u32[]{:S(2)}) copy-start(f32[1024]{0:T(1024)} %copy-done.12) | copy-start | bytes 12292
  921.2 243.5 %copy-start.15 = (f32[512,2]{0,1:T(2,128)S(1)}, f32[512,2]{0,1:T(2,128)}, u32[]{:S(2)}) copy-start(f32[512,2]{0,1:T(2,128)} %copy-done.14) | copy-start | bytes 12292
  921.2 243.5 %copy-start.23 = (f32[512,2]{0,1:T(2,128)S(1)}, f32[512,2]{0,1:T(2,128)}, u32[]{:S(2)}) copy-start(f32[512,2]{0,1:T(2,128)} %copy-done.22) | copy-start | bytes 12292
  921.2 243.5 %copy-start.25 = (f32[512,2]{0,1:T(2,128)S(1)}, f32[512,2]{0,1:T(2,128)}, u32[]{:S(2)}) copy-start(f32[512,2]{0,1:T(2,128)} %copy-done.24) | copy-start | bytes 12292
  (18 other events, 125.7 us)
Sparse Core Ops, SparseCore 0:
  56.3 53.9 all-gather.7
  112.5 45.2 all-gather.9
  159.9 36.7 all-gather.11
  268.5 53.0 reduce-scatter.7
  323.9 50.7 all-gather.15
  376.1 55.2 all-gather.13
  433.8 50.5 all-gather.17
  520.7 52.7 reduce-scatter.11
  581.9 56.7 all-gather.19
  642.4 72.4 reduce-scatter.19
  719.2 71.6 reduce-scatter.17
  880.3 111.2 all-reduce.13
  996.3 56.2 reduce-scatter.15
  1054.7 53.3 reduce-scatter.13
  1110.3 54.2 reduce-scatter.9
